TPU v7x, 512 devices: a whole 4x8x8 slice. The times are simulated.
512 devices in a mesh: row: 32 (over z_hi, y, core), col: 16 (over x, z_lo).
Axes of the slice: x: 4, y: 8, z: 8 (z_hi: 2, z_lo: 4; z = z_hi * 4 + z_lo), core: 2. Of those that a mesh axis runs over, the one named last changes fastest.
Arguments:
- coherency: bfloat16 [8, 16, 1, 16, 512, 512], P(None, None, None, 'col', 'row'), may hold values from -6 to 6
- visibilities: float32 [8, 1, 16, 512, 512], P(None, None, 'col', 'row'), may hold values from -24 to 24
- flags: int32 [1, 16, 512, 512], P(None, 'col', 'row'), may hold values 0 or 1
- gains: float32 [8, 16, 16, 512], P(None, None, 'col', 'row'), may hold values from -4 to 4
Outputs:
- residual: float32 [8, 1, 16, 512, 512], P(None, None, 'col', 'row')
- new_gains: float32 [8, 16, 16, 512], P(None, None, 'col', 'row')
Inputs may be any that keep to these rules, and one draw needn't show every extreme that they name: `flags`: 1 keeps a sample, 0 drops it.
All inputs are finite; a program needn't handle non-finite values. No bound on the sum of `flags` on one device may be relied on, other than what follows from the above.
Results may differ from a plain program's by a relative error of at most 0.0003.
Values sent between devices are 32-bit elements; how exact they have to be, the bound alone decides.
A program may use at most 128 MiB of HBM per device.

v0:
```python
import jax
import jax.numpy as jnp
from jax import lax
from jax.sharding import PartitionSpec as P

epsilon = 1e-06


def broadcast(shard, axis, root):
    mine = lax.axis_index(axis) == root
    return lax.psum(jnp.where(mine, shard, jnp.zeros_like(shard)), axis)


def split_planes(packed, widen):
    return [
        [
            (widen(packed[4 * line + 2 * column]), widen(packed[4 * line + 2 * column + 1]))
            for column in range(2)
        ]
        for line in range(2)
    ]


def stack_planes(matrix):
    return jnp.stack(
        [
            matrix[line][column][part]
            for line in range(2)
            for column in range(2)
            for part in range(2)
        ],
        axis=0,
    )


def complex_mul(first, second):
    return (
        first[0] * second[0] - first[1] * second[1],
        first[0] * second[1] + first[1] * second[0],
    )


def complex_mul_conj(first, second):
    return (
        first[0] * second[0] + first[1] * second[1],
        first[1] * second[0] - first[0] * second[1],
    )


def complex_add(first, second):
    return (first[0] + second[0], first[1] + second[1])


def matrix_product(first, second):
    return [
        [
            complex_add(
                complex_mul(first[line][0], second[0][column]),
                complex_mul(first[line][1], second[1][column]),
            )
            for column in range(2)
        ]
        for line in range(2)
    ]


def product_herm(first, second):
    return [
        [
            complex_add(
                complex_mul_conj(first[line][0], second[column][0]),
                complex_mul_conj(first[line][1], second[column][1]),
            )
            for column in range(2)
        ]
        for line in range(2)
    ]


def herm_product(first, second):
    return [
        [
            complex_add(
                complex_mul_conj(second[0][column], first[0][line]),
                complex_mul_conj(second[1][column], first[1][line]),
            )
            for column in range(2)
        ]
        for line in range(2)
    ]


def sum_squares(matrix):
    total = matrix[0][0][0] * matrix[0][0][0]
    for line in range(2):
        for column in range(2):
            for part in range(2):
                if line + column + part > 0:
                    total = total + matrix[line][column][part] * matrix[line][column][part]
    return total


def block_terms(row_jones, sky_block, col_jones, observed, weight):
    quota = col_jones.shape[3]
    channels = col_jones.shape[2]
    directions = col_jones.shape[1]

    def widen_row(plane):
        return jnp.repeat(jnp.swapaxes(plane, 0, 1), quota, axis=1)[None, :, :]

    def widen_col(plane):
        return plane.reshape(channels * quota)[None, None, :]

    def direction_parts(index):
        row_one = lax.dynamic_index_in_dim(row_jones, index, 1, keepdims=False)
        col_one = lax.dynamic_index_in_dim(col_jones, index, 1, keepdims=False)
        sky_one = lax.dynamic_index_in_dim(sky_block, index, 1, keepdims=False)
        left = split_planes(row_one, widen_row)
        right = split_planes(col_one, widen_col)
        sky = split_planes(sky_one, lambda plane: plane.astype(jnp.float32))
        front = matrix_product(left, sky)
        return (front, right, sky)

    def model_step(total, index):
        front, right, sky = direction_parts(index)
        return (total + stack_planes(product_herm(front, right)), None)

    model_sum, _ = lax.scan(
        model_step, jnp.zeros(observed.shape, jnp.float32), jnp.arange(directions, dtype=jnp.int32)
    )
    residual = weight[None] * (observed - model_sum)
    error = split_planes(residual, lambda plane: plane)

    def gradient_step(carry, index):
        front, right, sky = direction_parts(index)
        behind = product_herm(sky, right)
        row_full = stack_planes(product_herm(error, behind))
        row_grad = -jnp.swapaxes(
            row_full.reshape(row_full.shape[:3] + (channels, quota)).sum(axis=(1, 4)), 1, 2
        )
        col_full = stack_planes(herm_product(error, front)).sum(axis=(1, 2))
        col_grad = -col_full.reshape(8, channels, quota)
        behind_weight = weight * sum_squares(behind)
        row_curv = jnp.swapaxes(
            behind_weight.reshape(behind_weight.shape[:2] + (channels, quota)).sum(axis=(0, 3)),
            0,
            1,
        )
        front_weight = (weight * sum_squares(front)).sum(axis=(0, 1))
        col_curv = front_weight.reshape(channels, quota)
        return (carry, (row_grad, row_curv, col_grad, col_curv))

    _, (row_grad, row_curv, col_grad, col_curv) = lax.scan(
        gradient_step, 0, jnp.arange(directions, dtype=jnp.int32)
    )
    row_grad = jnp.moveaxis(row_grad, 0, 1)
    col_grad = jnp.moveaxis(col_grad, 0, 1)
    return (residual, row_grad, row_curv[None], col_grad, col_curv[None])


def on_device(coherency, visibilities, flags, gains):
    row_count = lax.axis_size("row")
    column_count = lax.axis_size("col")
    ratio = row_count // column_count
    row_place = lax.axis_index("row")
    column_place = lax.axis_index("col")
    row_jones = lax.all_gather(gains, "col", axis=2, tiled=True)
    span = row_jones.shape[3]
    channels = row_jones.shape[2]
    every_jones = lax.all_gather(row_jones, "row", axis=3, tiled=True)
    col_jones = lax.dynamic_slice_in_dim(
        every_jones, column_place * (span * ratio), span * ratio, 3
    )
    width = col_jones.shape[3]
    rows = row_place * span + jnp.arange(span, dtype=jnp.int32)
    columns = column_place * width + jnp.arange(channels * width, dtype=jnp.int32) % width
    sky_block = coherency[:, :, :, 0]
    observed = visibilities[:, :, 0]
    weight = (
        flags[:, 0].astype(jnp.float32)
        * (rows[:, None] != columns[None, :]).astype(jnp.float32)[None]
    )
    residual, row_grad, row_curv, col_grad, col_curv = block_terms(
        row_jones, sky_block, col_jones, observed, weight
    )
    grad_rows, curv_rows = (
        lax.psum_scatter(row_grad, "col", scatter_dimension=2, tiled=True),
        lax.psum_scatter(row_curv, "col", scatter_dimension=2, tiled=True),
    )
    full_grad, full_curv = lax.psum((col_grad, col_curv), "row")
    offset = row_place % ratio * span
    piece_grad = lax.dynamic_slice_in_dim(full_grad, offset, span, 3)
    piece_curv = lax.dynamic_slice_in_dim(full_curv, offset, span, 3)
    owner_grad, owner_curv = (
        broadcast(piece_grad, "col", row_place // ratio),
        broadcast(piece_curv, "col", row_place // ratio),
    )
    owned_channels = gains.shape[2]
    grad_columns = lax.dynamic_slice_in_dim(
        owner_grad, column_place * owned_channels, owned_channels, 2
    )
    curv_columns = lax.dynamic_slice_in_dim(
        owner_curv, column_place * owned_channels, owned_channels, 2
    )
    total_grad = grad_rows + grad_columns
    total_curv = curv_rows + curv_columns
    new_gains = gains - total_grad / (total_curv + epsilon)
    return (residual[:, :, None], new_gains)


def solution(mesh):
    return jax.shard_map(
        on_device,
        mesh=mesh,
        in_specs=(
            P(None, None, None, "col", "row", None),
            P(None, None, "col", "row", None),
            P(None, "col", "row", None),
            P(None, None, "col", "row"),
        ),
        out_specs=(P(None, None, "col", "row", None), P(None, None, "col", "row")),
        check_vma=False,
    )
```

profile of v0, /device:TPU:6, one launch (start us, length us, event | category | flops | bytes accessed | tf_op | source)
XLA Modules:
  0.0 1827.5 jit_solution(16351258376733582019)
XLA Ops:
  7.2 49.0 %all_gather.6 = f32[8,16,16,16]{3,1,0,2:T(8,128)S(1)} all-gather(f32[8,16,1,16]{3,1,0,2:T(8,128)} %bitcast.933), channel_id=1, replica_groups=mesh['row'=32,'col'=16] {'col'}, dimensions={2}, use_global_device_ids=true | all-gather | bytes 139264 | tf_op jit(solution)/shard_map/all_gather | solution.py:167
  60.6 343.1 %all-gather.2.cloned.1.call-done = f32[8,16,16,512]{2,1,0,3:T(8,128)} async-done(((f32[8,16,16,16]{2,1,0,3:T(8,128)}), f32[8,16,16,512]{2,1,0,3:T(8,128)}) %all-gather.2.cloned.1.call-update) | async-done | bytes 4194320 | tf_op jit(solution)/shard_map/all_gather | solution.py:170
  407.5 139.1 %while.28 = (s32[]{:T(128)}, f32[8,1,16,512]{3,2,1,0:T(8,128)S(1)}, s32[16]{0:T(128)S(1)}, f32[8,16,16,16]{2,3,1,0:T(8,128)}, bf16[8,16,1,16,512]{4,3,2,1,0:T(8,...) while((s32[]{:T(128)}, f32[8,1,16,512]{3,2,1,0:T(8,128)S(1)}, ...), condition=%wide.region_1.2_spmd.clone, body=%wide.region_0.1_spmd.clone.sunk | while | flops 1179660 | bytes 3563937 | solution.py:128
  547.3 592.2 %while.27 = (s32[]{:T(128)}, f32[16,8,16,16]{3,0,1,2:T(8,128)}, f32[16,16,16]{2,0,1:T(8,128)}, f32[16,8,16,32]{3,0,1,2:T(8,128)}, f32[16,16,32]{2,0,1:T(8,128)},...) while((s32[]{:T(128)}, f32[16,8,16,16]{3,0,1,2:T(8,128)}, ...), condition=%wide.region_7.8_spmd, body=%wide.region_2.7_spmd.sunk | while | flops 3357962 | bytes 21361224 | solution.py:153
  555.3 2.9 dynamic_update_slice.22
  592.4 2.9 dynamic_update_slice.22
  629.4 2.9 dynamic_update_slice.22
  666.4 2.9 dynamic_update_slice.22
  703.4 2.9 dynamic_update_slice.22
  740.4 2.9 dynamic_update_slice.22
  777.4 2.9 dynamic_update_slice.22
  814.5 2.9 dynamic_update_slice.22
  851.5 2.9 dynamic_update_slice.22
  871.0 2.9 dynamic_update_slice.20
  888.5 2.9 dynamic_update_slice.22
  908.0 2.9 dynamic_update_slice.20
  945.1 2.9 dynamic_update_slice.20
  962.5 2.9 dynamic_update_slice.22
  982.1 2.9 dynamic_update_slice.20
  999.5 2.9 dynamic_update_slice.22
  1019.1 2.9 dynamic_update_slice.20
  1036.5 2.9 dynamic_update_slice.22
  1056.1 2.9 dynamic_update_slice.20
  1073.6 2.9 dynamic_update_slice.22
  1093.1 2.9 dynamic_update_slice.20
  1130.1 2.9 dynamic_update_slice.20
  1140.3 168.4 %psum.30 = f32[1,16,16,32]{3,1,0,2:T(8,128)S(1)} all-reduce(f32[1,16,16,32]{3,1,0,2:T(8,128)} %bitcast.936), channel_id=1, replica_groups=mesh['row'=32,'col'=16] {'row'}, use_global_device_ids=true, to_apply=%region_12.13 | all-reduce | flops 8192 | bytes 65536 | tf_op jit(solution)/shard_map/psum | solution.py:190
  1309.0 73.8 %psum.31 = f32[1,16,16,16]{3,1,0,2:T(8,128)S(1)} all-reduce(f32[1,16,16,16]{3,1,0,2:T(8,128)S(1)} %dynamic-slice_select_fusion.1), channel_id=1, replica_groups=mesh['row'=32,'col'=16] {'col'}, use_global_device_ids=true, to_apply=%region_13.14 | all-reduce | flops 4096 | bytes 32768 | tf_op jit(solution)/shard_map/psum | solution.py:11
  1382.7 94.9 %all-reduce.3.cloned.1.call-done = f32[8,16,16,32]{3,1,0,2:T(8,128)} async-done(((f32[8,16,16,32]{3,1,0,2:T(8,128)}), f32[8,16,16,32]{3,1,0,2:T(8,128)}) %all-reduce.3.cloned.1.call-update) | async-done | bytes 262160 | tf_op jit(solution)/shard_map/psum | solution.py:190
  1480.2 78.6 %reduce-scatter.5.cloned.1.call-done = f32[1,16,1,16]{3,1,0,2:T(8,128)} async-done(((f32[1,16,16,16]{3,1,0,2:T(8,128)}), f32[1,16,1,16]{3,1,0,2:T(8,128)}) %reduce-scatter.5.cloned.1.call-update) | async-done | bytes 1040 | tf_op jit(solution)/shard_map/reduce_scatter | solution.py:188
  1559.5 87.7 %reduce-scatter.3.cloned.1.call-done = f32[8,16,1,16]{3,1,0,2:T(8,128)} async-done(((f32[8,16,16,16]{3,1,0,2:T(8,128)}), f32[8,16,1,16]{3,1,0,2:T(8,128)}) %reduce-scatter.3.cloned.1.call-update) | async-done | bytes 8208 | tf_op jit(solution)/shard_map/reduce_scatter | solution.py:187
  1647.3 172.2 %all-reduce.5.cloned.1.call-done = f32[8,16,16,16]{3,1,0,2:T(8,128)} async-done(((f32[8,16,16,16]{3,1,0,2:T(8,128)}), f32[8,16,16,16]{3,1,0,2:T(8,128)}) %all-reduce.5.cloned.1.call-update) | async-done | bytes 131088 | tf_op jit(solution)/shard_map/psum | solution.py:11
  (3121 shorter events, 600.7 us)
Async XLA Ops:
  7.2 396.5 %all-gather.2.cloned.1.call-start = ((), (), s32[]{:S(2)}) async-start(), calls=%async_computation.2 | async-start | bytes 34603008 | tf_op jit(solution)/shard_map/all_gather | solution.py:170
  58.3 1419.4 %all-reduce.3.cloned.1.call-start = ((), (), s32[]{:S(2)}) async-start(), calls=%async_computation.4 | async-start | bytes 2097152 | tf_op jit(solution)/shard_map/psum | solution.py:190
  407.5 139.1 %copy-start.38 = (f32[8,1,1,16,512]{4,3,2,1,0:T(8,128)S(1)}, f32[8,1,1,16,512]{4,3,2,1,0:T(8,128)}, u32[]{:S(2)}) copy-start(f32[8,1,1,16,512]{4,3,2,1,0:T(8,128)} %param.9) | copy-start | bytes 786436
  584.4 14.6 copy-start.4
  584.4 14.6 copy-start.6
  584.4 14.6 copy-start.8
  584.4 14.6 copy-start.16
  621.4 14.6 copy-start.4
  621.4 14.6 copy-start.6
  621.4 14.6 copy-start.8
  621.4 14.6 copy-start.16
  658.4 14.6 copy-start.4
  658.4 14.6 copy-start.6
  658.4 14.6 copy-start.8
  658.4 14.6 copy-start.16
  695.4 14.6 copy-start.4
  695.4 14.6 copy-start.6
  695.4 14.6 copy-start.8
  695.4 14.6 copy-start.16
  732.4 14.6 copy-start.4
  732.4 14.6 copy-start.6
  732.5 14.6 copy-start.8
  732.5 14.6 copy-start.16
  769.5 14.6 copy-start.4
  806.5 14.6 copy-start.4
  806.5 14.6 copy-start.6
  806.5 14.6 copy-start.8
  806.5 14.6 copy-start.16
  1139.6 419.3 %reduce-scatter.5.cloned.1.call-start = ((), (), s32[]{:S(2)}) async-start(), calls=%async_computation.6 | async-start | bytes 139264 | tf_op jit(solution)/shard_map/reduce_scatter | solution.py:188
  1140.3 506.9 %reduce-scatter.3.cloned.1.call-start = ((), (), s32[]{:S(2)}) async-start(), calls=%async_computation.3 | async-start | bytes 1114112 | tf_op jit(solution)/shard_map/reduce_scatter | solution.py:187
  1308.8 510.7 %copy-start.39 = (f32[8,16,1,16]{3,2,1,0:T(1,128)S(1)}, f32[8,16,1,16]{3,2,1,0:T(1,128)}, u32[]{:S(2)}) copy-start(f32[8,16,1,16]{3,2,1,0:T(1,128)} %param.11) | copy-start | bytes 24580
  1308.8 510.7 %all-reduce.5.cloned.1.call-start = ((), (), s32[]{:S(2)}) async-start(), calls=%async_computation.5 | async-start | bytes 2097152 | tf_op jit(solution)/shard_map/psum | solution.py:11
  (569 other events, 3545.8 us)
Sparse Core Ops, SparseCore 0:
  58.4 345.2 all-gather.1
  1139.7 337.9 all-reduce.2
  1480.7 78.0 reduce-scatter.4
  1561.5 85.7 reduce-scatter.2
  1650.3 169.1 all-reduce.4
where the time goes:
time: 1860 us; the launch traced here: 1830 us
  waiting for transfers between devices  777 us (42%)
  local copies, waits for them, and re-layouts  502 us (27%)
  blocking collectives  291 us (16%)
  other arithmetic  162 us (9%)
  loops' own time  81.4 us (4%)
    all_gather x1, waiting for transfers between devices, on_device(): every_jones = lax.all_gather(row_jones, 'row', axis=3, tiled=True)  343 us
    psum x1, waiting for transfers between devices, broadcast(): return lax.psum(jnp.where(mine, shard, jnp.zeros_like(shard)), axis)  172 us
    psum x1, blocking collectives, on_device(): full_grad, full_curv = lax.psum((col_grad, col_curv), 'row')  168 us
    dynamic_update_slice x112, local copies, waits for them, and re-layouts, block_terms(): lax.scan(gradient_step, 0, jnp.arange(directions, dtype=jnp.int32))  145 us
    convert_element_type x256, local copies, waits for them, and re-layouts, direction_parts(): sky = split_planes(sky_one, lambda plane: plane.astype(jnp.float32))  113 us
    while x336, other arithmetic  101 us
    psum x1, waiting for transfers between devices, on_device(): full_grad, full_curv = lax.psum((col_grad, col_curv), 'row')  94.9 us
    reduce_scatter x1, waiting for transfers between devices, on_device(): lax.psum_scatter(row_grad, 'col', scatter_dimension=2, tiled=True)  87.7 us
  transfers between devices with their start and end apart: 5, of which 5 were waited for; matrix products, arithmetic and copies ran while one was open for 0% of the time, Pallas kernels for 0%

commit v1 on v0

v1 whole, which is shorter than its diff:
```python
import functools

import jax
import jax.numpy as jnp
from jax import lax
from jax.experimental import pallas as pl
from jax.experimental.pallas import tpu as pltpu
from jax.sharding import PartitionSpec as P

epsilon = 1e-06
MESH = pl.DeviceIdType.MESH
LANES = 128
QUOTA = 32
FAN = LANES // QUOTA
SLOT = 24
USED = 18
BLOCK = 16


def mul(first, second):
    out = []
    for a in range(2):
        for b in range(2):
            re = im = None
            for k in range(2):
                fr, fi = first[4 * a + 2 * k], first[4 * a + 2 * k + 1]
                sr, si = second[4 * k + 2 * b], second[4 * k + 2 * b + 1]
                r, i = fr * sr - fi * si, fr * si + fi * sr
                re, im = (r, i) if re is None else (re + r, im + i)
            out += [re, im]
    return out


def mul_herm(first, second, total=None):
    out = []
    for a in range(2):
        for c in range(2):
            re = im = None
            if total is not None:
                re, im = total[4 * a + 2 * c], total[4 * a + 2 * c + 1]
            for b in range(2):
                fr, fi = first[4 * a + 2 * b], first[4 * a + 2 * b + 1]
                sr, si = second[4 * c + 2 * b], second[4 * c + 2 * b + 1]
                r, i = fr * sr + fi * si, fi * sr - fr * si
                re, im = (r, i) if re is None else (re + r, im + i)
            out += [re, im]
    return out


def herm_mul(first, second):
    out = []
    for a in range(2):
        for c in range(2):
            re = im = None
            for b in range(2):
                fr, fi = first[4 * b + 2 * a], first[4 * b + 2 * a + 1]
                sr, si = second[4 * b + 2 * c], second[4 * b + 2 * c + 1]
                r, i = sr * fr + si * fi, si * fr - sr * fi
                re, im = (r, i) if re is None else (re + r, im + i)
            out += [re, im]
    return out


def squares(planes):
    total = planes[0] * planes[0]
    for plane in planes[1:]:
        total = total + plane * plane
    return total


def swap_bits(x, row_bit, lane_bit, row_of, block_of):
    row_high = (row_of >> row_bit) & 1
    lane_high = (block_of >> lane_bit) & 1
    rows, lanes = 1 << row_bit, 16 << lane_bit
    up = pltpu.roll(pltpu.roll(x, 8 - rows, 0), lanes, 1)
    down = pltpu.roll(pltpu.roll(x, rows, 0), LANES - lanes, 1)
    return jnp.where(row_high == lane_high, x, jnp.where(row_high == 0, up, down))


def place_of(low):
    return (low % 2) * 4 + ((low // 4) % 2) * 2 + (low // 2) % 2


SWAPS = ((2, 0), (1, 2), (0, 1))


def kernel(
    n_col, n_dir, n_p,
    sky_ref, seen_ref, flag_ref, gain_ref, res_out, gain_out,
    sky_v, seen_v, flag_v, gain_v, wide_v, send_v, row_v, col_v, part_v, left_v, right_v,
    front_v, wide_sky_v, res_v, prod_v, colsum_v, rmsg_v, cmsg_v, sib_v, rin_v, cin_v, new_v,
    in_sem, r_send, c_send, r_recv, c_recv, relay_send, relay_recv, sib_send, sib_recv,
    ro_send, ro_recv, co_send, co_recv, out_sem,
):
    i, k = lax.axis_index("row"), lax.axis_index("col")
    m, h = i // 2, i % 2
    groups = n_col // FAN
    first_group = k // FAN
    sibling = 2 * m + (1 - h)
    alone = k == m
    f32, bf16 = jnp.float32, jnp.bfloat16

    def lanes_of(g):
        return pl.ds(pl.multiple_of(g * LANES, LANES), LANES)

    def rows_at(ref, start, size):
        return ref.at[pl.ds(pl.multiple_of(start, 8), size)]

    gain_copy = pltpu.make_async_copy(gain_ref, gain_v, in_sem.at[0])
    gain_copy.start()
    seen_copy = pltpu.make_async_copy(seen_ref, seen_v, in_sem.at[1])
    flag_copy = pltpu.make_async_copy(flag_ref, flag_v, in_sem.at[2])

    def sky_copy(g):
        return pltpu.make_async_copy(
            sky_ref.at[:, :, :, lanes_of(g)], sky_v.at[g], in_sem.at[3 + g]
        )

    barrier = pltpu.get_barrier_semaphore()

    def signal(row, col):
        pl.semaphore_signal(barrier, inc=1, device_id=(row, col), device_id_type=MESH)

    signal(sibling, k)

    @pl.loop(1, n_col)
    def _(o):
        signal(i, (k + o) % n_col)

    @pl.loop(0, n_col)
    def _(o):
        c = (m + o) % n_col

        @pl.when(jnp.logical_not(jnp.logical_and(alone, c == m)))
        def _():
            signal(2 * k + h, c)

    for t in range(groups):
        sky_copy((first_group + t) % groups).start()
    seen_copy.start()
    flag_copy.start()

    gain_copy.wait()
    wide_v[...] = jnp.zeros_like(wide_v)
    wide_v[:, 0:16] = gain_v[...]
    own = wide_v[pl.ds(0, BLOCK, stride=8), :]
    for j in range(1, 8):
        own = own + pltpu.roll(wide_v[pl.ds(j, BLOCK, stride=8), :], 16 * j, 1)
    send_v[...] = own

    pl.semaphore_wait(barrier, 2 * n_col - alone.astype(jnp.int32))

    def col_row(c, half):
        return (((c // FAN) * 2 + half) * FAN + c % FAN) * BLOCK

    def send_row(c):
        pltpu.make_async_remote_copy(
            src_ref=send_v, dst_ref=rows_at(row_v, k * BLOCK, BLOCK),
            send_sem=r_send.at[0], recv_sem=r_recv.at[k // FAN],
            device_id=(i, c), device_id_type=MESH,
        ).start()

    def send_col(target):
        pltpu.make_async_remote_copy(
            src_ref=send_v, dst_ref=rows_at(col_v, col_row(k, h), BLOCK),
            send_sem=c_send.at[0], recv_sem=c_recv.at[k // FAN],
            device_id=(2 * target + h, m), device_id_type=MESH,
        ).start()

    pltpu.make_async_copy(
        send_v, rows_at(row_v, k * BLOCK, BLOCK), r_recv.at[k // FAN]
    ).start()

    @pl.when(alone)
    def _():
        pltpu.make_async_copy(
            send_v, rows_at(col_v, col_row(k, h), BLOCK), c_recv.at[k // FAN]
        ).start()

    @pl.loop(1, FAN)
    def _(o):
        send_row(first_group * FAN + (k + o) % FAN)

    @pl.loop(1, n_col)
    def _(o):
        send_col((m + o) % n_col)

    @pl.when(jnp.logical_not(alone))
    def _():
        send_col(m)

    @pl.loop(FAN, n_col)
    def _(o):
        send_row(((first_group + groups - o // FAN) % groups) * FAN + (k + o) % FAN)

    def relay(g, half):
        block = rows_at(col_v, (g * 2 + half) * FAN * BLOCK, FAN * BLOCK)
        return pltpu.make_async_remote_copy(
            src_ref=block, dst_ref=block,
            send_sem=relay_send.at[g], recv_sem=relay_recv.at[g],
            device_id=(sibling, k), device_id_type=MESH,
        )

    def pass_on(g):
        block = rows_at(col_v, (g * 2 + h) * FAN * BLOCK, FAN * BLOCK)
        pltpu.make_async_copy(block, block, c_recv.at[g]).wait()
        relay(g, h).start()

    def exchange(g):
        return pltpu.make_async_remote_copy(
            src_ref=rows_at(cmsg_v, (g * 2 + 1 - h) * FAN * SLOT, FAN * SLOT),
            dst_ref=rows_at(sib_v, g * FAN * SLOT, FAN * SLOT),
            send_sem=sib_send.at[g], recv_sem=sib_recv.at[g],
            device_id=(sibling, k), device_id_type=MESH,
        )

    def row_out(c):
        return pltpu.make_async_remote_copy(
            src_ref=rows_at(rmsg_v, c * SLOT, USED), dst_ref=rows_at(rin_v, k * SLOT, USED),
            send_sem=ro_send.at[c], recv_sem=ro_recv.at[k],
            device_id=(i, c), device_id_type=MESH,
        )

    def cmsg_row(c):
        return (((c // FAN) * 2 + h) * FAN + c % FAN) * SLOT

    def col_out(c):
        return pltpu.make_async_remote_copy(
            src_ref=rows_at(cmsg_v, cmsg_row(c), USED), dst_ref=rows_at(cin_v, m * SLOT, USED),
            send_sem=co_send.at[c], recv_sem=co_recv.at[m],
            device_id=(2 * k + h, c), device_id_type=MESH,
        )

    def send_cols(g):
        exchange(g).wait_recv()
        base = pl.multiple_of((g * 2 + h) * FAN * SLOT, 8)
        span = pl.ds(base, FAN * SLOT)
        cmsg_v[span] = cmsg_v[span] + sib_v[pl.ds(pl.multiple_of(g * FAN * SLOT, 8), FAN * SLOT)]

        @pl.loop(0, FAN)
        def _(o):
            c = g * FAN + o

            @pl.when(jnp.logical_and(alone, c == m))
            def _():
                pltpu.make_async_copy(
                    rows_at(cmsg_v, cmsg_row(c), USED), rows_at(cin_v, m * SLOT, USED),
                    co_recv.at[m],
                ).start()

            @pl.when(jnp.logical_not(jnp.logical_and(alone, c == m)))
            def _():
                col_out(c).start()

    row_of = lax.broadcasted_iota(jnp.int32, (8, LANES), 0)
    lane_of = lax.broadcasted_iota(jnp.int32, (8, LANES), 1)
    block_of = lane_of // 16
    low_row = lax.broadcasted_iota(jnp.int32, (16, LANES), 0)
    low_lane = lax.broadcasted_iota(jnp.int32, (16, LANES), 1)
    widen = jnp.where(
        jnp.logical_and(low_lane // QUOTA == low_row % FAN, low_row < 3 * FAN), 1.0, 0.0
    ).astype(bf16)
    sum_row = lax.broadcasted_iota(jnp.int32, (8, 2 * LANES), 0)
    sum_lane = lax.broadcasted_iota(jnp.int32, (8, 2 * LANES), 1)
    gather = jnp.where((sum_lane % LANES) // QUOTA == sum_row, 1.0, 0.0).astype(bf16)

    part_v[3 * FAN * BLOCK :] = jnp.zeros((FAN * BLOCK, LANES), f32)

    pass_on(first_group)

    @pl.loop(0, groups)
    def _(t):
        g = (first_group + t) % groups

        @pl.when(t + 1 < groups)
        def _():
            pass_on((first_group + t + 1) % groups)

        relay(g, 1 - h).wait_recv()
        block = rows_at(row_v, g * FAN * BLOCK, FAN * BLOCK)
        pltpu.make_async_copy(block, block, r_recv.at[g]).wait()

        for r in range(BLOCK):
            x = col_v[pl.ds(g * (2 * FAN * BLOCK) + r, 8, stride=BLOCK), :]
            for row_bit, lane_bit in SWAPS:
                x = swap_bits(x, row_bit, lane_bit, row_of, block_of)
            right_v[8 * r : 8 * r + 8, :] = x

        value = row_v[pl.ds(pl.multiple_of(g * FAN * BLOCK, 8), FAN * BLOCK), :]
        high = value.astype(bf16).astype(f32)
        rest = value - high
        middle = rest.astype(bf16).astype(f32)
        part_v[0 : FAN * BLOCK] = high
        part_v[FAN * BLOCK : 2 * FAN * BLOCK] = middle
        part_v[2 * FAN * BLOCK : 3 * FAN * BLOCK] = rest - middle
        for r in range(BLOCK):
            x = part_v[pl.ds(r, 16, stride=BLOCK), :]
            left_v[r * LANES : (r + 1) * LANES, :] = lax.dot_general(
                x.T.astype(bf16), widen, (((1,), (0,)), ((), ())), preferred_element_type=f32
            )

        @pl.when(t == 0)
        def _():
            seen_copy.wait()
            flag_copy.wait()

        sky_copy(g).wait()

        def right_of(d):
            at = (d // 8) * 8 + place_of(d % 8)
            return [
                jnp.broadcast_to(right_v[pl.ds(plane * n_dir + at, 1), :], (8, LANES))
                for plane in range(8)
            ]

        def model_step(d, total):
            right = right_of(d)
            sky = [sky_v[g, plane, d].astype(f32) for plane in range(8)]
            new = []
            for half in range(2):
                part = [plane[8 * half : 8 * half + 8] for plane in sky]
                left = [
                    left_v[pl.ds(pl.multiple_of((plane * n_dir + d) * n_p + 8 * half, 8), 8), :]
                    for plane in range(8)
                ]
                front = mul(left, part)
                for plane in range(8):
                    front_v[plane, d, 8 * half : 8 * half + 8] = front[plane]
                    wide_sky_v[plane, d, 8 * half : 8 * half + 8] = part[plane]
                new += mul_herm(front, right, total[8 * half : 8 * half + 8])
            return tuple(new)

        zero = jnp.zeros((8, LANES), f32)
        model = lax.fori_loop(0, n_dir, model_step, (zero,) * 16)

        @pl.when(t > 0)
        def _():
            send_cols((first_group + t + groups - 1) % groups)

        lanes = lanes_of(g)
        weight, error = [], []
        for half in range(2):
            rows = i * n_p + 8 * half + row_of
            columns = k * QUOTA + lane_of % QUOTA
            kept = flag_v[8 * half : 8 * half + 8, lanes].astype(f32)
            kept = kept * (rows != columns).astype(f32)
            weight.append(kept)
            for plane in range(8):
                seen = seen_v[plane, 8 * half : 8 * half + 8, lanes]
                value = kept * (seen - model[8 * half + plane])
                error.append(value)
                res_v[plane, 8 * half : 8 * half + 8, lanes] = value
        pltpu.make_async_copy(
            res_v.at[:, :, lanes], res_out.at[:, :, lanes], out_sem.at[g]
        ).start()

        def sum_step(d, carry):
            right = right_of(d)
            rows, cols = [], None
            for half in range(2):
                wrong = error[8 * half : 8 * half + 8]
                sky = [wide_sky_v[plane, d, 8 * half : 8 * half + 8] for plane in range(8)]
                front = [front_v[plane, d, 8 * half : 8 * half + 8] for plane in range(8)]
                behind = mul_herm(sky, right)
                rows.append(mul_herm(wrong, behind) + [weight[half] * squares(behind)])
                col = herm_mul(wrong, front) + [weight[half] * squares(front)]
                cols = col if cols is None else [a + b for a, b in zip(cols, col)]
            at = pl.ds(pl.multiple_of(d * n_p, 16), n_p)
            for plane in range(9):
                x = jnp.concatenate([rows[0][plane], rows[1][plane]], axis=0)
                high = x.astype(bf16)
                prod_v[plane, at, 0:LANES] = high
                prod_v[plane, at, LANES : 2 * LANES] = (x - high.astype(f32)).astype(bf16)
                colsum_v[plane, d] = cols[plane]
            return carry

        lax.fori_loop(0, n_dir, sum_step, 0)

        for plane in range(9):
            x = lax.dot_general(
                gather, prod_v[plane], (((1,), (1,)), ((), ())), preferred_element_type=f32
            )
            for high in range(n_dir // 8):
                rmsg_v[pl.ds(g * FAN * SLOT + 2 * plane + high, FAN, stride=SLOT), :] = x[
                    0:FAN, high * LANES : (high + 1) * LANES
                ]

        @pl.loop(0, FAN)
        def _(o):
            c = g * FAN + o

            @pl.when(c == k)
            def _():
                pltpu.make_async_copy(
                    rows_at(rmsg_v, k * SLOT, USED), rows_at(rin_v, k * SLOT, USED), ro_recv.at[k]
                ).start()

            @pl.when(c != k)
            def _():
                row_out(c).start()

        for plane in range(9):
            for high in range(n_dir // 8):
                items = [None] * 8
                for low in range(8):
                    items[place_of(low)] = colsum_v[plane, 8 * high + low]
                for bit in range(3):
                    up = ((row_of >> bit) & 1) == 1
                    items = [
                        jnp.where(up, b, a) + pltpu.roll(jnp.where(up, a, b), 1 << bit, 0)
                        for a, b in zip(items[0::2], items[1::2])
                    ]
                x = items[0]
                for row_bit, lane_bit in SWAPS:
                    x = swap_bits(x, row_bit, lane_bit, row_of, block_of)
                cmsg_v[pl.ds(g * 2 * FAN * SLOT + 2 * plane + high, 8, stride=SLOT), :] = x
        exchange(g).start()

    send_cols((first_group + groups - 1) % groups)

    def add_up(buffer, sems, source, total):
        at = rows_at(buffer, source * SLOT, USED)
        pltpu.make_async_copy(at, at, sems.at[source]).wait()
        start = pl.multiple_of(source * SLOT, 8)
        return tuple(
            part + buffer[pl.ds(start + 8 * n, size), :]
            for n, (part, size) in enumerate(zip(total, (8, 8, 2)))
        )

    def add_step(o, total):
        total = add_up(rin_v, ro_recv, (k + o) % n_col, total)
        return add_up(cin_v, co_recv, (m + o) % n_col, total)

    zero = jnp.zeros((8, LANES), f32)
    top, bottom, curvature = lax.fori_loop(
        0, n_col, add_step, (zero, zero, jnp.zeros((2, LANES), f32))
    )
    divisor = jnp.where(
        row_of % 2 == 0,
        jnp.broadcast_to(curvature[0:1], (8, LANES)),
        jnp.broadcast_to(curvature[1:2], (8, LANES)),
    ) + epsilon
    fresh = send_v[...] + jnp.concatenate([top / divisor, bottom / divisor], axis=0)
    for j in range(8):
        wide_v[pl.ds(j, BLOCK, stride=8), :] = fresh if j == 0 else pltpu.roll(fresh, LANES - 16 * j, 1)
    new_v[...] = wide_v[:, 0:16]
    new_copy = pltpu.make_async_copy(new_v, gain_out, out_sem.at[groups])
    new_copy.start()

    sent = rows_at(row_v, 0, (n_col - 1) * BLOCK)
    pltpu.make_async_copy(sent, sent, r_send.at[0]).wait()

    @pl.when(alone)
    def _():
        sent = rows_at(row_v, 0, (n_col - 1) * BLOCK)
        pltpu.make_async_copy(sent, sent, c_send.at[0]).wait()

    @pl.when(jnp.logical_not(alone))
    def _():
        sent = rows_at(row_v, 0, n_col * BLOCK)
        pltpu.make_async_copy(sent, sent, c_send.at[0]).wait()

    @pl.loop(0, groups)
    def _(g):
        relay(g, h).wait_send()
        exchange(g).wait_send()
        lanes = lanes_of(g)
        pltpu.make_async_copy(
            res_v.at[:, :, lanes], res_out.at[:, :, lanes], out_sem.at[g]
        ).wait()

    @pl.loop(0, n_col)
    def _(c):
        @pl.when(c != k)
        def _():
            row_out(c).wait_send()

        @pl.when(jnp.logical_not(jnp.logical_and(alone, c == m)))
        def _():
            col_out(c).wait_send()

    new_copy.wait()


def on_device(coherency, visibilities, flags, gains):
    n_col = lax.axis_size("col")
    n_dir, n_p, width = coherency.shape[1], coherency.shape[4], coherency.shape[5]
    groups = width // LANES
    sky = coherency.reshape(8, n_dir, n_p, width)
    seen = visibilities.reshape(8, n_p, width)
    flag = flags.reshape(n_p, width)
    mine = gains.reshape(8 * n_dir, n_p)
    f32, bf16 = jnp.float32, jnp.bfloat16
    any_spec = pl.BlockSpec(memory_space=pl.ANY)
    dma = pltpu.SemaphoreType.DMA
    residual, fresh = pl.pallas_call(
        functools.partial(kernel, n_col, n_dir, n_p),
        out_shape=(
            jax.ShapeDtypeStruct(seen.shape, f32),
            jax.ShapeDtypeStruct(mine.shape, f32),
        ),
        in_specs=[any_spec] * 4,
        out_specs=(any_spec, any_spec),
        scratch_shapes=[
            pltpu.VMEM((groups, 8, n_dir, n_p, LANES), bf16),
            pltpu.VMEM(seen.shape, f32),
            pltpu.VMEM(flag.shape, jnp.int32),
            pltpu.VMEM(mine.shape, f32),
            pltpu.VMEM((8 * n_dir, LANES), f32),
            pltpu.VMEM((BLOCK, LANES), f32),
            pltpu.VMEM((n_col * BLOCK, LANES), f32),
            pltpu.VMEM((2 * n_col * BLOCK, LANES), f32),
            pltpu.VMEM((4 * FAN * BLOCK, LANES), f32),
            pltpu.VMEM((8 * n_dir * n_p, LANES), f32),
            pltpu.VMEM((8 * n_dir, LANES), f32),
            pltpu.VMEM((8, n_dir, n_p, LANES), f32),
            pltpu.VMEM((8, n_dir, n_p, LANES), f32),
            pltpu.VMEM(seen.shape, f32),
            pltpu.VMEM((9, n_dir * n_p, 2 * LANES), bf16),
            pltpu.VMEM((9, n_dir, 8, LANES), f32),
            pltpu.VMEM((n_col * SLOT, LANES), f32),
            pltpu.VMEM((2 * n_col * SLOT, LANES), f32),
            pltpu.VMEM((n_col * SLOT, LANES), f32),
            pltpu.VMEM((n_col * SLOT, LANES), f32),
            pltpu.VMEM((n_col * SLOT, LANES), f32),
            pltpu.VMEM(mine.shape, f32),
            dma((3 + groups,)),
            dma((1,)),
            dma((1,)),
            dma((groups,)),
            dma((groups,)),
            dma((groups,)),
            dma((groups,)),
            dma((groups,)),
            dma((groups,)),
            dma((n_col,)),
            dma((n_col,)),
            dma((n_col,)),
            dma((n_col,)),
            dma((groups + 1,)),
        ],
        compiler_params=pltpu.CompilerParams(
            collective_id=0, has_side_effects=True, vmem_limit_bytes=56 * 1024 * 1024
        ),
    )(sky, seen, flag, mine)
    return residual.reshape(visibilities.shape), fresh.reshape(gains.shape)


def solution(mesh):
    return jax.shard_map(
        on_device,
        mesh=mesh,
        in_specs=(
            P(None, None, None, "col", "row", None),
            P(None, None, "col", "row", None),
            P(None, "col", "row", None),
            P(None, None, "col", "row"),
        ),
        out_specs=(P(None, None, "col", "row", None), P(None, None, "col", "row")),
        check_vma=False,
    )
```

time: 1860 us -> 57.4 us (0.03)
  the two profiles are of different devices: /device:TPU:6 before, /device:TPU:79 now
where the time goes in v1:
time: 57.4 us; the launch traced here: 57.1 us
  Pallas kernels  53.3 us (93%)
  local copies, waits for them, and re-layouts  3.14 us (5%)
  between operations  0.64 us (1%)
    pallas_call x1, Pallas kernels, on_device(): pl.pallas_call(functools.partial(kernel, n_col, n_dir, n_p), out_shape=(j...  53.3 us
    unnamed x2, local copies, waits for them, and re-layouts  3.14 us

profile of v1, /device:TPU:79, one launch (start us, length us, event | category | flops | bytes accessed | tf_op | source)
XLA Modules:
  0.0 57.1 jit_solution(1722792667668775601)
XLA Ops:
  0.6 53.3 %shard_map.59 = (f32[8,16,512]{2,1,0:T(8,128)}, f32[128,16]{1,0:T(8,128)}) custom-call(bf16[8,16,16,512]{3,2,1,0:T(8,128)(2,1)} %bitcast.10, f32[8,16,512]{2,1,0:T(8,128)} %bitcast.11, s32[16,512]{1,0:T(8,128)} %bitcast.15, f32[128,16]{1,0:T(8,128)} %bitcast.13), custom_call_target="tpu_custom_call" | custom-call | tf_op jit(solution)/shard_map/pallas_call | solution.py:496
  54.0 1.7 %copy.10 = f32[8,1,1,16,512]{4,3,2,1,0:T(8,128)} copy(f32[8,1,1,16,512]{4,3,2,1,0:T(8,128)} %bitcast.12) | data formatting | bytes 524288
  55.7 1.5 %copy.11 = f32[8,16,1,16]{3,2,1,0:T(1,128)} copy(f32[8,16,1,16]{3,2,1,0:T(1,128)} %bitcast.14) | data formatting | bytes 16384

commit v2 on v1

--- a/solution.py
+++ b/solution.py
@@ -13,6 +13,8 @@
 QUOTA = 32
 FAN = LANES // QUOTA
 SLOT = 24
+MODEL_UNROLL = 4
+SUM_UNROLL = 4
 USED = 18
 BLOCK = 16
 
@@ -88,9 +90,9 @@
     n_col, n_dir, n_p,
     sky_ref, seen_ref, flag_ref, gain_ref, res_out, gain_out,
     sky_v, seen_v, flag_v, gain_v, wide_v, send_v, row_v, col_v, part_v, left_v, right_v,
-    front_v, wide_sky_v, res_v, prod_v, colsum_v, rmsg_v, cmsg_v, sib_v, rin_v, cin_v, new_v,
+    front_v, wide_sky_v, res_v, prod_v, colsum_v, rmsg_v, cmsg_v, sib_v, rin_v, mid_v, cin_v, new_v,
     in_sem, r_send, c_send, r_recv, c_recv, relay_send, relay_recv, sib_send, sib_recv,
-    ro_send, ro_recv, co_send, co_recv, out_sem,
+    ro_send, ro_recv, co_send, mid_recv, on_send, cin_recv, out_sem,
 ):
     i, k = lax.axis_index("row"), lax.axis_index("col")
     m, h = i // 2, i % 2
@@ -177,20 +179,17 @@
             send_v, rows_at(col_v, col_row(k, h), BLOCK), c_recv.at[k // FAN]
         ).start()
 
-    @pl.loop(1, FAN)
-    def _(o):
+    for o in range(1, FAN):
         send_row(first_group * FAN + (k + o) % FAN)
 
-    @pl.loop(1, n_col)
-    def _(o):
+    for o in range(1, n_col):
         send_col((m + o) % n_col)
 
     @pl.when(jnp.logical_not(alone))
     def _():
         send_col(m)
 
-    @pl.loop(FAN, n_col)
-    def _(o):
+    for o in range(FAN, n_col):
         send_row(((first_group + groups - o // FAN) % groups) * FAN + (k + o) % FAN)
 
     def relay(g, half):
@@ -226,31 +225,62 @@
 
     def col_out(c):
         return pltpu.make_async_remote_copy(
+            src_ref=rows_at(cmsg_v, cmsg_row(c), USED), dst_ref=rows_at(mid_v, k * SLOT, USED),
+            send_sem=co_send.at[c], recv_sem=mid_recv.at[k],
+            device_id=(i, c), device_id_type=MESH,
+        )
+
+    def col_on(source):
+        return pltpu.make_async_remote_copy(
+            src_ref=rows_at(mid_v, source * SLOT, USED), dst_ref=rows_at(cin_v, m * SLOT, USED),
+            send_sem=on_send.at[source], recv_sem=cin_recv.at[m],
+            device_id=(2 * source + h, k), device_id_type=MESH,
+        )
+
+    def col_direct(c):
+        return pltpu.make_async_remote_copy(
             src_ref=rows_at(cmsg_v, cmsg_row(c), USED), dst_ref=rows_at(cin_v, m * SLOT, USED),
-            send_sem=co_send.at[c], recv_sem=co_recv.at[m],
+            send_sem=co_send.at[c], recv_sem=cin_recv.at[m],
             device_id=(2 * k + h, c), device_id_type=MESH,
         )
 
-    def send_cols(g):
+    def send_cols(g, last):
         exchange(g).wait_recv()
         base = pl.multiple_of((g * 2 + h) * FAN * SLOT, 8)
         span = pl.ds(base, FAN * SLOT)
         cmsg_v[span] = cmsg_v[span] + sib_v[pl.ds(pl.multiple_of(g * FAN * SLOT, 8), FAN * SLOT)]
 
-        @pl.loop(0, FAN)
-        def _(o):
+        for o in range(FAN):
             c = g * FAN + o
-
-            @pl.when(jnp.logical_and(alone, c == m))
+            stays = jnp.logical_and(alone, c == k) if last else c == k
+            target, place, sems = (cin_v, m, cin_recv) if last else (mid_v, k, mid_recv)
+
+            @pl.when(stays)
             def _():
                 pltpu.make_async_copy(
-                    rows_at(cmsg_v, cmsg_row(c), USED), rows_at(cin_v, m * SLOT, USED),
-                    co_recv.at[m],
+                    rows_at(cmsg_v, cmsg_row(c), USED), rows_at(target, place * SLOT, USED),
+                    sems.at[place],
                 ).start()
 
-            @pl.when(jnp.logical_not(jnp.logical_and(alone, c == m)))
+            @pl.when(jnp.logical_not(stays))
             def _():
-                col_out(c).start()
+                (col_direct if last else col_out)(c).start()
+
+    def send_on(t):
+        for o in range(FAN):
+            source = ((first_group + groups - t) % groups) * FAN + o
+            at = rows_at(mid_v, source * SLOT, USED)
+            pltpu.make_async_copy(at, at, mid_recv.at[source]).wait()
+
+            @pl.when(source == m)
+            def _():
+                pltpu.make_async_copy(
+                    rows_at(mid_v, m * SLOT, USED), rows_at(cin_v, m * SLOT, USED), cin_recv.at[m]
+                ).start()
+
+            @pl.when(source != m)
+            def _():
+                col_on(source).start()
 
     row_of = lax.broadcasted_iota(jnp.int32, (8, LANES), 0)
     lane_of = lax.broadcasted_iota(jnp.int32, (8, LANES), 1)
@@ -293,11 +323,13 @@
         part_v[0 : FAN * BLOCK] = high
         part_v[FAN * BLOCK : 2 * FAN * BLOCK] = middle
         part_v[2 * FAN * BLOCK : 3 * FAN * BLOCK] = rest - middle
-        for r in range(BLOCK):
-            x = part_v[pl.ds(r, 16, stride=BLOCK), :]
-            left_v[r * LANES : (r + 1) * LANES, :] = lax.dot_general(
-                x.T.astype(bf16), widen, (((1,), (0,)), ((), ())), preferred_element_type=f32
-            )
+        left_v[...] = jnp.dot(
+            jnp.concatenate(
+                [part_v[pl.ds(r, 16, stride=BLOCK), :].T for r in range(BLOCK)], axis=0
+            ).astype(bf16),
+            widen,
+            preferred_element_type=f32,
+        )
 
         @pl.when(t == 0)
         def _():
@@ -313,29 +345,32 @@
                 for plane in range(8)
             ]
 
-        def model_step(d, total):
-            right = right_of(d)
-            sky = [sky_v[g, plane, d].astype(f32) for plane in range(8)]
-            new = []
-            for half in range(2):
-                part = [plane[8 * half : 8 * half + 8] for plane in sky]
-                left = [
-                    left_v[pl.ds(pl.multiple_of((plane * n_dir + d) * n_p + 8 * half, 8), 8), :]
-                    for plane in range(8)
-                ]
-                front = mul(left, part)
-                for plane in range(8):
-                    front_v[plane, d, 8 * half : 8 * half + 8] = front[plane]
-                    wide_sky_v[plane, d, 8 * half : 8 * half + 8] = part[plane]
-                new += mul_herm(front, right, total[8 * half : 8 * half + 8])
-            return tuple(new)
+        def model_step(n, total):
+            for o in range(MODEL_UNROLL):
+                d = n * MODEL_UNROLL + o
+                right = right_of(d)
+                sky = [sky_v[g, plane, d].astype(f32) for plane in range(8)]
+                new = []
+                for half in range(2):
+                    part = [plane[8 * half : 8 * half + 8] for plane in sky]
+                    left = [
+                        left_v[pl.ds(pl.multiple_of((plane * n_dir + d) * n_p + 8 * half, 8), 8), :]
+                        for plane in range(8)
+                    ]
+                    front = mul(left, part)
+                    for plane in range(8):
+                        front_v[plane, d, 8 * half : 8 * half + 8] = front[plane]
+                        wide_sky_v[plane, d, 8 * half : 8 * half + 8] = part[plane]
+                    new += mul_herm(front, right, total[8 * half : 8 * half + 8])
+                total = tuple(new)
+            return total
 
         zero = jnp.zeros((8, LANES), f32)
-        model = lax.fori_loop(0, n_dir, model_step, (zero,) * 16)
+        model = lax.fori_loop(0, n_dir // MODEL_UNROLL, model_step, (zero,) * 16)
 
         @pl.when(t > 0)
         def _():
-            send_cols((first_group + t + groups - 1) % groups)
+            send_cols((first_group + t + groups - 1) % groups, False)
 
         lanes = lanes_of(g)
         weight, error = [], []
@@ -354,50 +389,29 @@
             res_v.at[:, :, lanes], res_out.at[:, :, lanes], out_sem.at[g]
         ).start()
 
-        def sum_step(d, carry):
-            right = right_of(d)
-            rows, cols = [], None
-            for half in range(2):
-                wrong = error[8 * half : 8 * half + 8]
-                sky = [wide_sky_v[plane, d, 8 * half : 8 * half + 8] for plane in range(8)]
-                front = [front_v[plane, d, 8 * half : 8 * half + 8] for plane in range(8)]
-                behind = mul_herm(sky, right)
-                rows.append(mul_herm(wrong, behind) + [weight[half] * squares(behind)])
-                col = herm_mul(wrong, front) + [weight[half] * squares(front)]
-                cols = col if cols is None else [a + b for a, b in zip(cols, col)]
-            at = pl.ds(pl.multiple_of(d * n_p, 16), n_p)
-            for plane in range(9):
-                x = jnp.concatenate([rows[0][plane], rows[1][plane]], axis=0)
-                high = x.astype(bf16)
-                prod_v[plane, at, 0:LANES] = high
-                prod_v[plane, at, LANES : 2 * LANES] = (x - high.astype(f32)).astype(bf16)
-                colsum_v[plane, d] = cols[plane]
+        def sum_step(n, carry):
+            for o in range(SUM_UNROLL):
+                d = n * SUM_UNROLL + o
+                right = right_of(d)
+                rows, cols = [], None
+                for half in range(2):
+                    wrong = error[8 * half : 8 * half + 8]
+                    sky = [wide_sky_v[plane, d, 8 * half : 8 * half + 8] for plane in range(8)]
+                    front = [front_v[plane, d, 8 * half : 8 * half + 8] for plane in range(8)]
+                    behind = mul_herm(sky, right)
+                    rows.append(mul_herm(wrong, behind) + [weight[half] * squares(behind)])
+                    col = herm_mul(wrong, front) + [weight[half] * squares(front)]
+                    cols = col if cols is None else [a + b for a, b in zip(cols, col)]
+                at = pl.ds(pl.multiple_of(d * n_p, 16), n_p)
+                for plane in range(9):
+                    x = jnp.concatenate([rows[0][plane], rows[1][plane]], axis=0)
+                    high = x.astype(bf16)
+                    prod_v[plane, at, 0:LANES] = high
+                    prod_v[plane, at, LANES : 2 * LANES] = (x - high.astype(f32)).astype(bf16)
+                    colsum_v[plane, d] = cols[plane]
             return carry
 
-        lax.fori_loop(0, n_dir, sum_step, 0)
-
-        for plane in range(9):
-            x = lax.dot_general(
-                gather, prod_v[plane], (((1,), (1,)), ((), ())), preferred_element_type=f32
-            )
-            for high in range(n_dir // 8):
-                rmsg_v[pl.ds(g * FAN * SLOT + 2 * plane + high, FAN, stride=SLOT), :] = x[
-                    0:FAN, high * LANES : (high + 1) * LANES
-                ]
-
-        @pl.loop(0, FAN)
-        def _(o):
-            c = g * FAN + o
-
-            @pl.when(c == k)
-            def _():
-                pltpu.make_async_copy(
-                    rows_at(rmsg_v, k * SLOT, USED), rows_at(rin_v, k * SLOT, USED), ro_recv.at[k]
-                ).start()
-
-            @pl.when(c != k)
-            def _():
-                row_out(c).start()
+        lax.fori_loop(0, n_dir // SUM_UNROLL, sum_step, 0)
 
         for plane in range(9):
             for high in range(n_dir // 8):
@@ -416,7 +430,36 @@
                 cmsg_v[pl.ds(g * 2 * FAN * SLOT + 2 * plane + high, 8, stride=SLOT), :] = x
         exchange(g).start()
 
-    send_cols((first_group + groups - 1) % groups)
+        for plane in range(9):
+            x = lax.dot_general(
+                gather, prod_v[plane], (((1,), (1,)), ((), ())), preferred_element_type=f32
+            )
+            for high in range(n_dir // 8):
+                rmsg_v[pl.ds(g * FAN * SLOT + 2 * plane + high, FAN, stride=SLOT), :] = x[
+                    0:FAN, high * LANES : (high + 1) * LANES
+                ]
+
+        for o in range(FAN):
+            c = g * FAN + o
+
+            @pl.when(c == k)
+            def _():
+                pltpu.make_async_copy(
+                    rows_at(rmsg_v, k * SLOT, USED), rows_at(rin_v, k * SLOT, USED), ro_recv.at[k]
+                ).start()
+
+            @pl.when(c != k)
+            def _():
+                row_out(c).start()
+
+        @pl.when(jnp.logical_and(t > 1, t < groups - 1))
+        def _():
+            send_on(t - 2)
+
+    last_group = (first_group + groups - 1) % groups
+    send_cols(last_group, True)
+    for t in range(max(groups - 3, 0), groups - 1):
+        send_on(t)
 
     def add_up(buffer, sems, source, total):
         at = rows_at(buffer, source * SLOT, USED)
@@ -429,7 +472,7 @@
 
     def add_step(o, total):
         total = add_up(rin_v, ro_recv, (k + o) % n_col, total)
-        return add_up(cin_v, co_recv, (m + o) % n_col, total)
+        return add_up(cin_v, cin_recv, (m + o) % n_col, total)
 
     zero = jnp.zeros((8, LANES), f32)
     top, bottom, curvature = lax.fori_loop(
@@ -475,9 +518,18 @@
         def _():
             row_out(c).wait_send()
 
-        @pl.when(jnp.logical_not(jnp.logical_and(alone, c == m)))
-        def _():
-            col_out(c).wait_send()
+        last = c // FAN == last_group
+        stays = jnp.where(last, jnp.where(alone, c, -1), c) == k
+
+        @pl.when(jnp.logical_not(stays))
+        def _():
+            col_direct(c).wait_send()
+
+        late = (c // FAN + groups - 1) % groups == first_group
+
+        @pl.when(jnp.logical_not(jnp.logical_or(late, c == m)))
+        def _():
+            col_on(c).wait_send()
 
     new_copy.wait()
 
@@ -523,6 +575,7 @@
             pltpu.VMEM((n_col * SLOT, LANES), f32),
             pltpu.VMEM((n_col * SLOT, LANES), f32),
             pltpu.VMEM((n_col * SLOT, LANES), f32),
+            pltpu.VMEM((n_col * SLOT, LANES), f32),
             pltpu.VMEM(mine.shape, f32),
             dma((3 + groups,)),
             dma((1,)),
@@ -537,6 +590,8 @@
             dma((n_col,)),
             dma((n_col,)),
             dma((n_col,)),
+            dma((n_col,)),
+            dma((n_col,)),
             dma((groups + 1,)),
         ],
         compiler_params=pltpu.CompilerParams(

time: 57.4 us -> 52.5 us (0.915)
  the two profiles are of different devices: /device:TPU:79 before, /device:TPU:5 now
where the time goes in v2:
time: 52.5 us; the launch traced here: 52.3 us
  Pallas kernels  48.5 us (92%)
  local copies, waits for them, and re-layouts  3.14 us (6%)
  between operations  0.64 us (1%)
    pallas_call x1, Pallas kernels, on_device(): pl.pallas_call(functools.partial(kernel, n_col, n_dir, n_p), out_shape=(j...  48.5 us
    unnamed x2, local copies, waits for them, and re-layouts  3.14 us

profile of v2, /device:TPU:5, one launch (start us, length us, event | category | flops | bytes accessed | tf_op | source)
XLA Modules:
  0.0 52.3 jit_solution(12738031245589222697)
XLA Ops:
  0.6 48.5 %shard_map.59 = (f32[8,16,512]{2,1,0:T(8,128)}, f32[128,16]{1,0:T(8,128)}) custom-call(bf16[8,16,16,512]{3,2,1,0:T(8,128)(2,1)} %bitcast.10, f32[8,16,512]{2,1,0:T(8,128)} %bitcast.11, s32[16,512]{1,0:T(8,128)} %bitcast.15, f32[128,16]{1,0:T(8,128)} %bitcast.13), custom_call_target="tpu_custom_call" | custom-call | tf_op jit(solution)/shard_map/pallas_call | solution.py:548
  49.1 1.7 %copy.10 = f32[8,1,1,16,512]{4,3,2,1,0:T(8,128)} copy(f32[8,1,1,16,512]{4,3,2,1,0:T(8,128)} %bitcast.12) | data formatting | bytes 524288
  50.8 1.5 %copy.11 = f32[8,16,1,16]{3,2,1,0:T(1,128)} copy(f32[8,16,1,16]{3,2,1,0:T(1,128)} %bitcast.14) | data formatting | bytes 16384

commit v3 on v2

--- a/solution.py
+++ b/solution.py
@@ -13,8 +13,8 @@
 QUOTA = 32
 FAN = LANES // QUOTA
 SLOT = 24
-MODEL_UNROLL = 4
-SUM_UNROLL = 4
+MODEL_UNROLL = 8
+SUM_UNROLL = 8
 USED = 18
 BLOCK = 16
 
@@ -179,15 +179,15 @@
             send_v, rows_at(col_v, col_row(k, h), BLOCK), c_recv.at[k // FAN]
         ).start()
 
-    for o in range(1, FAN):
-        send_row(first_group * FAN + (k + o) % FAN)
-
     for o in range(1, n_col):
         send_col((m + o) % n_col)
 
     @pl.when(jnp.logical_not(alone))
     def _():
         send_col(m)
+
+    for o in range(1, FAN):
+        send_row(first_group * FAN + (k + o) % FAN)
 
     for o in range(FAN, n_col):
         send_row(((first_group + groups - o // FAN) % groups) * FAN + (k + o) % FAN)
@@ -452,13 +452,13 @@
             def _():
                 row_out(c).start()
 
-        @pl.when(jnp.logical_and(t > 1, t < groups - 1))
+        @pl.when(t > 1)
         def _():
             send_on(t - 2)
 
     last_group = (first_group + groups - 1) % groups
     send_cols(last_group, True)
-    for t in range(max(groups - 3, 0), groups - 1):
+    for t in range(max(groups - 2, 0), groups - 1):
         send_on(t)
 
     def add_up(buffer, sems, source, total):
@@ -532,6 +532,21 @@
             col_on(c).wait_send()
 
     new_copy.wait()
+
+
+def hand_over(res_ref, gain_ref, res_out, gain_out, res_v, gain_v, sems):
+    pairs = [(gain_ref, gain_v, gain_out)]
+    for n in range(0, 8, 2):
+        pairs.append((res_ref.at[n : n + 2], res_v.at[n : n + 2], res_out.at[n : n + 2]))
+    first = [pltpu.make_async_copy(a, b, sems.at[n]) for n, (a, b, _) in enumerate(pairs)]
+    second = [pltpu.make_async_copy(b, c, sems.at[5 + n]) for n, (_, b, c) in enumerate(pairs)]
+    for copy in first:
+        copy.start()
+    for before, after in zip(first, second):
+        before.wait()
+        after.start()
+    for copy in second:
+        copy.wait()
 
 
 def on_device(coherency, visibilities, flags, gains):
@@ -598,6 +613,17 @@
             collective_id=0, has_side_effects=True, vmem_limit_bytes=56 * 1024 * 1024
         ),
     )(sky, seen, flag, mine)
+    residual, fresh = pl.pallas_call(
+        hand_over,
+        out_shape=(
+            jax.ShapeDtypeStruct(seen.shape, f32),
+            jax.ShapeDtypeStruct(mine.shape, f32),
+        ),
+        in_specs=[any_spec] * 2,
+        out_specs=(any_spec, any_spec),
+        scratch_shapes=[pltpu.VMEM(seen.shape, f32), pltpu.VMEM(mine.shape, f32), dma((10,))],
+        compiler_params=pltpu.CompilerParams(vmem_limit_bytes=56 * 1024 * 1024),
+    )(residual, fresh)
     return residual.reshape(visibilities.shape), fresh.reshape(gains.shape)
 
 

time: 52.5 us -> 50.3 us (0.958)
  the two profiles are of different devices: /device:TPU:5 before, /device:TPU:6 now
where the time goes in v3:
time: 50.3 us; the launch traced here: 50.1 us
  Pallas kernels  49.4 us (98%)
  between operations  0.64 us (1%)
    pallas_call x1, Pallas kernels, on_device(): pl.pallas_call(functools.partial(kernel, n_col, n_dir, n_p), out_shape=(j...  47.7 us
    pallas_call x1, Pallas kernels, on_device(): pl.pallas_call(hand_over, out_shape=(jax.ShapeDtypeStruct(seen.shape, f32...  1.68 us

profile of v3, /device:TPU:6, one launch (start us, length us, event | category | flops | bytes accessed | tf_op | source)
XLA Modules:
  0.0 50.1 jit_solution(12704836620643550184)
XLA Ops:
  0.6 47.7 %shard_map.59 = (f32[8,16,512]{2,1,0:T(8,128)}, f32[128,16]{1,0:T(8,128)}) custom-call(bf16[8,16,16,512]{3,2,1,0:T(8,128)(2,1)} %bitcast.10, f32[8,16,512]{2,1,0:T(8,128)} %bitcast.11, s32[16,512]{1,0:T(8,128)} %bitcast.13, f32[128,16]{1,0:T(8,128)} %bitcast.12), custom_call_target="tpu_custom_call" | custom-call | tf_op jit(solution)/shard_map/pallas_call | solution.py:563
  48.4 1.7 %shard_map.60 = (f32[8,16,512]{2,1,0:T(8,128)}, f32[128,16]{1,0:T(8,128)}) custom-call(f32[8,16,512]{2,1,0:T(8,128)} %get-tuple-element.6.res_ref, f32[128,16]{1,0:T(8,128)} %get-tuple-element.7.gain_ref), custom_call_target="tpu_custom_call" | custom-call | tf_op jit(solution)/shard_map/pallas_call | solution.py:616

commit v4 on v3

--- a/solution.py
+++ b/solution.py
@@ -123,19 +123,16 @@
     def signal(row, col):
         pl.semaphore_signal(barrier, inc=1, device_id=(row, col), device_id_type=MESH)
 
+    for o in range(1, n_col):
+        signal(2 * k + h, (m + o) % n_col)
+
+    @pl.when(jnp.logical_not(alone))
+    def _():
+        signal(2 * k + h, m)
+
+    for o in range(1, n_col):
+        signal(i, (k + o) % n_col)
     signal(sibling, k)
-
-    @pl.loop(1, n_col)
-    def _(o):
-        signal(i, (k + o) % n_col)
-
-    @pl.loop(0, n_col)
-    def _(o):
-        c = (m + o) % n_col
-
-        @pl.when(jnp.logical_not(jnp.logical_and(alone, c == m)))
-        def _():
-            signal(2 * k + h, c)
 
     for t in range(groups):
         sky_copy((first_group + t) % groups).start()

time: 50.3 us -> 49.8 us (0.990)
  no operation moved by 1% of the time
where the time goes in v4:
time: 49.8 us; the launch traced here: 49.6 us
  Pallas kernels  49 us (98%)
  between operations  0.64 us (1%)
    pallas_call x1, Pallas kernels, on_device(): pl.pallas_call(functools.partial(kernel, n_col, n_dir, n_p), out_shape=(j...  47.3 us
    pallas_call x1, Pallas kernels, on_device(): pl.pallas_call(hand_over, out_shape=(jax.ShapeDtypeStruct(seen.shape, f32...  1.68 us

profile of v4, /device:TPU:6, one launch (start us, length us, event | category | flops | bytes accessed | tf_op | source)
XLA Modules:
  0.0 49.6 jit_solution(3006867273704345203)
XLA Ops:
  0.6 47.3 %shard_map.59 = (f32[8,16,512]{2,1,0:T(8,128)}, f32[128,16]{1,0:T(8,128)}) custom-call(bf16[8,16,16,512]{3,2,1,0:T(8,128)(2,1)} %bitcast.10, f32[8,16,512]{2,1,0:T(8,128)} %bitcast.11, s32[16,512]{1,0:T(8,128)} %bitcast.13, f32[128,16]{1,0:T(8,128)} %bitcast.12), custom_call_target="tpu_custom_call" | custom-call | tf_op jit(solution)/shard_map/pallas_call | solution.py:560
  48.0 1.7 %shard_map.60 = (f32[8,16,512]{2,1,0:T(8,128)}, f32[128,16]{1,0:T(8,128)}) custom-call(f32[8,16,512]{2,1,0:T(8,128)} %get-tuple-element.6.res_ref, f32[128,16]{1,0:T(8,128)} %get-tuple-element.7.gain_ref), custom_call_target="tpu_custom_call" | custom-call | tf_op jit(solution)/shard_map/pallas_call | solution.py:613
